TPU v7x, 32 devices: a whole 2x2x4 slice. The times are simulated.
32 devices in a mesh: row: 4 (over y, x), col: 8 (over z, core).
Axes of the slice: x: 2, y: 2, z: 4, core: 2. Of those that a mesh axis runs over, the one named last changes fastest.
Arguments:
- beats: bfloat16 [65536, 128], P(('row', 'col')), may hold values from -6 to 6
- track_marks: int32 [65536], P(('row', 'col')), may hold values 0 or 1
- valid_beats: int32 [32], replicated, may hold values from 64 to 2048, as said below
- pairing: int32 [2, 32], replicated, may hold values from 0 to 31, as said below
Outputs:
- profile: float32 [65536], P(('row', 'col'))
Inputs may be any that keep to these rules, and one draw needn't show every extreme that they name: `valid_beats`: each segment has at least 64 valid beats; some segment is full in every draw. pairing[0] pairs the segments of each grid column among themselves and pairing[1] those of each grid row; each row of pairing is an involution without fixed points.
All inputs are finite; a program needn't handle non-finite values. No bound on the sum of `track_marks` on one device may be relied on, other than what follows from the above.
Results may differ from a plain program's by a relative error of at most 0.0003.
Values may be sent and summed in bfloat16 or wider, within the bound.
A program may use at most 128 MiB of HBM per device.

v0:
```python
import jax
import jax.numpy as jnp
from jax import lax
from jax.sharding import PartitionSpec as P

WIDTH = 128
SPAN = 64


CEIL = 4.0


def from_behind(block, axis, distance):
    devices = range(lax.axis_size(axis))
    route = [(i - distance, i) for i in devices if i - distance in devices]
    return lax.ppermute(block, axis, route)


def window_sum(values, count):
    total = values[0:count]
    for shift in range(1, SPAN):
        total = total + values[shift : shift + count]
    return total


def diagonal_window(gram):
    layered = gram
    window = 1
    offset = 0
    result = None
    while window <= SPAN:
        if SPAN & window:
            result = layered
            offset = offset + window
        if window * 2 <= SPAN:
            layered = layered[:-window, :-window] + layered[window:, window:]
        window = window * 2
    return result


def masked_block(
    left_ext,
    left_norm,
    left_live,
    left_pos,
    right_ext,
    right_first,
    right_norm,
    right_live,
    right_pos,
    left_count,
    right_count,
):
    right_rows = lax.dynamic_slice_in_dim(right_ext, right_first, right_count + SPAN - 1, 0)
    block_rows = min(512, left_count)
    block_total = left_count // block_rows

    def one_block(index):
        start = index * block_rows
        rows = lax.dynamic_slice_in_dim(left_ext, start, block_rows + SPAN - 1, 0)
        gram = lax.dot_general(
            rows, right_rows, (((1,), (1,)), ((), ())), preferred_element_type=jnp.float32
        )
        dots = diagonal_window(gram)
        norm_part = lax.dynamic_slice_in_dim(left_norm, start, block_rows, 0)
        live_part = lax.dynamic_slice_in_dim(left_live, start, block_rows, 0)
        pos_part = lax.dynamic_slice_in_dim(left_pos, start, block_rows, 0)
        dist = (norm_part[:, None] + right_norm[None, :] - 2.0 * dots) / (SPAN * WIDTH)
        allowed = (
            (live_part[:, None] > 0.5)
            & (right_live[None, :] > 0.5)
            & (jnp.abs(pos_part[:, None] - right_pos[None, :]) >= SPAN // 2)
        )
        masked = jnp.where(allowed, dist, CEIL)
        return (jnp.min(masked, axis=1), jnp.min(masked, axis=0))

    across, down = lax.map(one_block, jnp.arange(block_total, dtype=jnp.int32))
    return (across.reshape(left_count), jnp.min(down, axis=0))


def fetch_partner(own_ext, own_flags, target, axis_name):
    span_rows = own_ext.shape[0]

    def select(carry, pieces):
        ext_piece, flag_piece = pieces
        count = ext_piece.shape[0] // span_rows
        inside = (target >= 0) & (target < count)
        offset = jnp.clip(target, 0, count - 1) * span_rows
        taken_ext = lax.dynamic_slice_in_dim(ext_piece, offset, span_rows, 0)
        taken_flags = lax.dynamic_slice_in_dim(flag_piece, offset, span_rows, 0)
        return (jnp.where(inside, taken_ext, carry[0]), jnp.where(inside, taken_flags, carry[1]))

    empty = (jnp.zeros_like(own_ext), jnp.zeros_like(own_flags))
    if axis_name == "row":
        return select(
            empty,
            (
                lax.all_gather(own_ext, "row", axis=0, tiled=True),
                lax.all_gather(own_flags, "row", axis=0, tiled=True),
            ),
        )
    return select(
        empty,
        (
            lax.all_gather(own_ext, "col", axis=0, tiled=True),
            lax.all_gather(own_flags, "col", axis=0, tiled=True),
        ),
    )


def send_minima(slots, axis_name):
    if axis_name == "row":
        return lax.all_to_all(slots, "row", split_axis=0, concat_axis=0, tiled=True)
    return lax.all_to_all(slots, "col", split_axis=0, concat_axis=0, tiled=True)


def meeting(own_ext, own_flags, own_norm, own_pos, partner, target, axis_name, seg_count):
    far_ext, far_flags = fetch_partner(own_ext, own_flags, target, axis_name)
    far_sq = jnp.sum(jnp.square(far_ext.astype(jnp.float32)), axis=1)
    far_norm = window_sum(far_sq, seg_count)
    offsets = jnp.arange(seg_count, dtype=jnp.int32)
    far_pos = partner * seg_count + offsets
    own_live = own_flags[:seg_count].astype(jnp.float32)
    far_live = far_flags[:seg_count].astype(jnp.float32)
    half_count = seg_count // 2
    lower = lax.axis_index(("row", "col")) < partner
    left_ext = jnp.where(lower, own_ext, far_ext)
    left_norm = jnp.where(lower, own_norm, far_norm)
    left_live = jnp.where(lower, own_live, far_live)
    left_pos = jnp.where(lower, own_pos, far_pos)
    right_first = jnp.where(lower, 0, half_count).astype(jnp.int32)
    right_ext = jnp.where(lower, far_ext, own_ext)
    right_norm = lax.dynamic_slice_in_dim(
        jnp.where(lower, far_norm, own_norm), right_first, half_count, 0
    )
    right_live = lax.dynamic_slice_in_dim(
        jnp.where(lower, far_live, own_live), right_first, half_count, 0
    )
    right_pos = lax.dynamic_slice_in_dim(
        jnp.where(lower, far_pos, own_pos), right_first, half_count, 0
    )
    across, down = masked_block(
        left_ext,
        left_norm,
        left_live,
        left_pos,
        right_ext,
        right_first,
        right_norm,
        right_live,
        right_pos,
        seg_count,
        half_count,
    )
    capped = jnp.full((half_count,), CEIL, jnp.float32)
    kept = jnp.where(lower, across, jnp.concatenate([capped, down]))
    outgoing = jnp.where(lower, jnp.concatenate([down, capped]), across)
    members = lax.axis_size("row") if axis_name == "row" else lax.axis_size("col")
    slot_ids = jnp.arange(members, dtype=jnp.int32)
    slots = jnp.where(slot_ids[:, None] == target, outgoing[None, :], CEIL)
    arrived = send_minima(slots, axis_name)
    return jnp.minimum(kept, jnp.min(arrived, axis=0))


def per_device(beats, track_marks, valid_beats, pairing):
    seg_count = beats.shape[0]
    col_count = lax.axis_size("col")
    total = valid_beats.shape[0]
    me = lax.axis_index("row") * col_count + lax.axis_index("col")
    marks = track_marks.astype(jnp.bfloat16)
    head_beats, head_marks = from_behind((beats[:SPAN], marks[:SPAN]), ("row", "col"), -1)
    own_ext = jnp.concatenate([beats, head_beats], 0)
    mark_ext = jnp.concatenate([marks, head_marks], 0).astype(jnp.float32)
    crossed = mark_ext[1 : 1 + seg_count]
    for shift in range(2, SPAN):
        crossed = crossed + mark_ext[shift : shift + seg_count]
    offsets = jnp.arange(seg_count, dtype=jnp.int32)
    valid_here = valid_beats[me]
    within = offsets + (SPAN - 1) < valid_here
    crossing = (valid_here == seg_count) & (me < total - 1)
    live = (within | crossing) & (crossed < 0.5)
    own_flags = jnp.concatenate([live.astype(jnp.bfloat16), jnp.zeros((SPAN,), jnp.bfloat16)], 0)
    own_sq = jnp.sum(jnp.square(own_ext.astype(jnp.float32)), axis=1)
    own_norm = window_sum(own_sq, seg_count)
    own_pos = me * seg_count + offsets
    first_partner = pairing[0, me]
    second_partner = pairing[1, me]
    first = meeting(
        own_ext,
        own_flags,
        own_norm,
        own_pos,
        first_partner,
        first_partner // col_count,
        "row",
        seg_count,
    )
    second = meeting(
        own_ext,
        own_flags,
        own_norm,
        own_pos,
        second_partner,
        second_partner % col_count,
        "col",
        seg_count,
    )
    return jnp.minimum(first, second)


def solution(mesh):
    placed = (P(("row", "col"), None), P(("row", "col")), P(), P())
    return jax.shard_map(
        per_device, mesh=mesh, in_specs=placed, out_specs=P(("row", "col")), check_vma=False
    )
```

profile of v0, /device:TPU:0, one launch (start us, length us, event | category | flops | bytes accessed | tf_op | source)
XLA Modules:
  0.0 197.4 jit_solution(3071285307573655187)
XLA Ops:
  7.3 1.3 collective-permute-start.1
  12.6 1.3 collective-permute-start
  13.9 1.4 constant_dynamic-slice_fusion
  22.4 1.3 dynamic_slice.77
  24.4 1.3 dynamic-slice
  25.6 1.3 dynamic-slice.1
  29.9 26.8 %all-reduce.5 = bf16[8448]{0:T(1024)(128)(2,1)S(1)} all-reduce(bf16[8448]{0:T(1024)(128)(2,1)S(1)} %dynamic-update-slice), channel_id=1, replica_groups=mesh['row'=4,'col'=8] {'row'}, use_global_device_ids=true, to_apply=%add.5 | all-reduce | flops 8448 | bytes 33792
  56.7 27.5 %all-reduce.6 = bf16[16896]{0:T(1024)(128)(2,1)S(1)} all-reduce(bf16[16896]{0:T(1024)(128)(2,1)S(1)} %dynamic-update-slice.1), channel_id=1, replica_groups=mesh['row'=4,'col'=8] {'col'}, use_global_device_ids=true, to_apply=%add.6 | all-reduce | flops 16896 | bytes 67584
  84.5 1.4 multiply_reduce_fusion.2
  85.9 19.8 %all-gather.5.cloned.1.call-done = bf16[16896,128]{1,0:T(8,128)(2,1)} async-done(((bf16[2112,128]{1,0:T(8,128)(2,1)}), bf16[16896,128]{1,0:T(8,128)(2,1)}) %all-gather.5.cloned.1.call-update) | async-done | bytes 4325392 | tf_op jit(solution)/shard_map/all_gather | solution.py:105
  105.7 1.6 broadcast_select_fusion
  108.7 33.5 %while.24 = (s32[]{:T(128)}, f32[4,512]{1,0:T(4,128)S(1)}, f32[4,1024]{1,0:T(4,128)S(1)}, s32[4]{0:T(128)S(1)}, f32[2048]{0:T(1024)S(1)}, /*index=5*/f32[1024]{0...) while((s32[]{:T(128)}, f32[4,512]{1,0:T(4,128)S(1)}, ...), condition=%wide.region_5.6_spmd, body=%wide.region_2.5_spmd.sunk | while | flops 169853776 | bytes 43548412 | solution.py:77
  115.1 1.8 fusion.41
  123.5 1.8 fusion.41
  131.9 1.8 fusion.41
  140.2 1.8 fusion.41
  142.9 3.5 %all-to-all-start = ((f32[4,1,2048]{2,1,0:T(1,128)}), f32[4,1,2048]{2,1,0:T(1,128)S(1)}, u32[]{:S(2)}, u32[]{:S(2)}) async-start(f32[4,1,2048]{2,1,0:T(1,128)} %broadcast_select_fusion.3), calls=%async_computation | async-start | bytes 65536 | tf_op jit(solution)/shard_map/all_to_all | solution.py:113
  146.5 33.4 %while.25 = (s32[]{:T(128)}, f32[4,512]{1,0:T(4,128)S(1)}, f32[4,1024]{1,0:T(4,128)S(1)}, s32[4]{0:T(128)S(1)}, f32[2048]{0:T(1024)S(1)}, /*index=5*/f32[1024]{0...) while((s32[]{:T(128)}, f32[4,512]{1,0:T(4,128)S(1)}, ...), condition=%wide.region_12.13_spmd, body=%wide.region_9.12_spmd.sunk | while | flops 169853776 | bytes 43548412 | solution.py:77
  152.9 1.8 fusion.45
  161.3 1.8 fusion.45
  169.6 1.8 fusion.45
  178.0 1.8 fusion.45
  180.7 3.4 %all-to-all-start.1 = ((f32[8,1,2048]{2,1,0:T(1,128)}), f32[8,1,2048]{2,1,0:T(1,128)S(1)}, u32[]{:S(2)}, u32[]{:S(2)}) async-start(f32[8,1,2048]{2,1,0:T(1,128)} %broadcast_select_fusion.2), calls=%async_computation.1 | async-start | bytes 131072 | tf_op jit(solution)/shard_map/all_to_all | solution.py:114
  184.1 5.8 %all-to-all-done.1 = f32[8,1,2048]{2,1,0:T(1,128)S(1)} async-done(((f32[8,1,2048]{2,1,0:T(1,128)}), f32[8,1,2048]{2,1,0:T(1,128)S(1)}, u32[]{:S(2)}, u32[]{:S(2)}) %all-to-all-start.1) | async-done | bytes 65568 | tf_op jit(solution)/shard_map/all_to_all | solution.py:114
  (161 shorter events, 56.5 us)
Async XLA Ops:
  6.5 79.4 %all-gather.3.cloned.1.call-start = ((), (), s32[]{:S(2)}) async-start(), calls=%async_computation.2 | async-start | bytes 2703360 | tf_op jit(solution)/shard_map/all_gather | solution.py:98
  7.3 3.1 %collective-permute-start.1 = (bf16[64,128]{1,0:T(8,128)(2,1)S(1)}, bf16[64,128]{1,0:T(8,128)(2,1)S(1)}, u32[]{:S(2)}, u32[]{:S(2)}) collective-permute-start(bf16[64,128]{1,0:T(8,128)(2,1)S(1)} %slice.914), channel_id=1, source_target_pairs={{1,0},{2,1},{3,2},{4,3},{5,4},{6,5},{7,6},{8,7},{9,8},{10,9},{11,1... | collective-permute-start | bytes 49160 | tf_op jit(solution)/shard_map/ppermute | solution.py:16
  10.3 0.8 copy-start
  11.2 94.5 %copy-start.1 = (bf16[2112,128]{1,0:T(8,128)(2,1)S(1)}, bf16[2112,128]{1,0:T(8,128)(2,1)}, u32[]{:S(2)}) copy-start(bf16[2112,128]{1,0:T(8,128)(2,1)} %copy-done) | copy-start | bytes 1622020
  11.2 94.5 %all-gather.5.cloned.1.call-start = ((), (), s32[]{:S(2)}) async-start(), calls=%async_computation.3 | async-start | bytes 4866048 | tf_op jit(solution)/shard_map/all_gather | solution.py:105
  12.6 15.8 %collective-permute-start = (bf16[64]{0:T(256)(128)(2,1)S(1)}, bf16[64]{0:T(256)(128)(2,1)S(1)}, u32[]{:S(2)}, u32[]{:S(2)}) collective-permute-start(bf16[64]{0:T(256)(128)(2,1)S(1)} %slice.1132), channel_id=1, source_target_pairs={{1,0},{2,1},{3,2},{4,3},{5,4},{6,5},{7,6},{8,7},{9,8},{10,9},{11,1... | collective-permute-start | bytes 392 | tf_op jit(solution)/shard_map/ppermute | solution.py:16
  142.9 37.8 %all-to-all-start = ((f32[4,1,2048]{2,1,0:T(1,128)}), f32[4,1,2048]{2,1,0:T(1,128)S(1)}, u32[]{:S(2)}, u32[]{:S(2)}) async-start(f32[4,1,2048]{2,1,0:T(1,128)} %broadcast_select_fusion.3), calls=%async_computation | async-start | bytes 65536 | tf_op jit(solution)/shard_map/all_to_all | solution.py:113
  180.7 9.2 %all-to-all-start.1 = ((f32[8,1,2048]{2,1,0:T(1,128)}), f32[8,1,2048]{2,1,0:T(1,128)S(1)}, u32[]{:S(2)}, u32[]{:S(2)}) async-start(f32[8,1,2048]{2,1,0:T(1,128)} %broadcast_select_fusion.2), calls=%async_computation.1 | async-start | bytes 131072 | tf_op jit(solution)/shard_map/all_to_all | solution.py:114
Sparse Core Ops, SparseCore 0:
  11.3 43.4 all-gather.2
  56.4 49.1 all-gather.4
where the time goes:
time: 198 us; the launch traced here: 197 us
  other arithmetic  57.6 us (29%)
  blocking collectives  54.3 us (27%)
  waiting for transfers between devices  27 us (14%)
  between operations  22.8 us (12%)
  local copies, waits for them, and re-layouts  16.1 us (8%)
  starting transfers between devices  9.47 us (5%)
  loops' own time  6.11 us (3%)
  matrix products  4.11 us (2%)
    unnamed x2, blocking collectives  54.3 us
    add x40, other arithmetic, diagonal_window(): layered = layered[:-window, :-window] + layered[window:, window:]  34.1 us
    all_gather x1, waiting for transfers between devices, fetch_partner(): lax.all_gather(own_ext, 'col', axis=0, tiled=True)  19.8 us
    reduce_min x8, other arithmetic, one_block(): return (jnp.min(masked, axis=1), jnp.min(masked, axis=0))  14.4 us
    another operation x2, loops' own time, masked_block(): across, down = lax.map(one_block, jnp.arange(block_total, dtype=jnp.int32))  6.11 us
    all_to_all x1, waiting for transfers between devices, send_minima(): return lax.all_to_all(slots, 'col', split_axis=0, concat_axis=0, tiled=True)  5.8 us
    dynamic_slice x8, local copies, waits for them, and re-layouts, masked_block(): across, down = lax.map(one_block, jnp.arange(block_total, dtype=jnp.int32))  5.33 us
    unnamed x13, local copies, waits for them, and re-layouts  5.12 us
  transfers between devices with their start and end apart: 6, of which 3 were waited for; matrix products, arithmetic and copies ran while one was open for 21% of the time, Pallas kernels for 0%

commit v1 on v0

v1 whole, which is shorter than its diff:
```python
import functools

import jax
import jax.numpy as jnp
from jax import lax
from jax.experimental import pallas as pl
from jax.experimental.pallas import tpu as pltpu
from jax.sharding import PartitionSpec as P

SPAN = 64
CEIL = 4.0
BIG = 1e9
LANES = 128
SUB = 8
HIGH = LANES // SUB
LEAD = 4


def from_behind(block, axis, distance):
    devices = range(lax.axis_size(axis))
    route = [(i - distance, i) for i in devices if i - distance in devices]
    return lax.ppermute(block, axis, route)


def window_sum(values, count):
    layered = values
    window = 1
    while window < SPAN:
        layered = layered[:-window] + layered[window:]
        window = window * 2
    return layered[:count]


def meet_kernel(
    rows, tiles, x_ref, y_ref, na_ref, nb_ref, pen_ref, ro_ref, co_ref,
    xf, yf, x8, y8, ga, gb, gc, a10, a11, a20, a21, a22, a23, nab, rm,
):
    width = x_ref.shape[1]
    x_rows = x8.shape[0]
    steps = (tiles + 8) // 4
    a1c = (a10, a11)
    a2c = (a20, a21, a22, a23)
    gram = (ga, gb)
    shift0 = 4 * steps
    chains = rows + 12
    half = chains // 2

    xf[...] = jnp.zeros_like(xf)
    xf[: x_ref.shape[0], :] = x_ref[...].astype(jnp.float32) * -2.0
    yf[:SUB, :] = jnp.zeros((SUB, width), jnp.float32)
    yf[SUB : SUB + y_ref.shape[0], :] = y_ref[...].astype(jnp.float32)
    for ref in (gc,) + a1c + a2c:
        ref[...] = jnp.zeros_like(ref)
    for ref in gram:
        ref[: LEAD * SUB, :] = jnp.zeros((LEAD * SUB, ref.shape[1]), jnp.float32)
    nab[...] = jnp.full_like(nab, BIG)
    nab[16 * SUB : (16 + rows) * SUB, :] = jnp.broadcast_to(na_ref[...], (rows * SUB, LANES))
    rm[...] = jnp.full_like(rm, BIG)

    part = x_rows // 10

    def fill_x(c, carry):
        start = pl.multiple_of(c * part, 16)
        piece = xf[pl.ds(start, part + SUB), :]
        for m in range(SUB):
            x8[pl.ds(start, part), m * width : (m + 1) * width] = piece[m : m + part].astype(jnp.bfloat16)
        return carry

    lax.fori_loop(0, 10, fill_x, 0)

    def fill_y(c, carry):
        pieces = [yf[pl.ds(pl.multiple_of(h * tiles * SUB + c * SUB, SUB), 2 * SUB), :] for h in range(HIGH)]
        start = pl.multiple_of(c * LANES, LANES)
        for m in range(SUB):
            whole = jnp.concatenate([p[m : m + SUB] for p in pieces], 0)
            y8[pl.ds(start, LANES), m * width : (m + 1) * width] = whole.astype(jnp.bfloat16)
        return carry

    lax.fori_loop(0, 4 * steps, fill_y, 0)

    def multiply(k, s):
        first = (4 * k + 2 * s) * LANES
        out = gram[k % 2]
        out[LEAD * SUB :, 2 * s * LANES : 2 * (s + 1) * LANES] = lax.dot_general(
            x8[...], y8[first : first + 2 * LANES, :], (((1,), (1,)), ((), ())),
            preferred_element_type=jnp.float32,
        )

    def combine(k, s, mins):
        g = gram[k % 2]
        last = k >= 2
        if last:
            nbs = [jnp.broadcast_to(nb_ref[4 * k - 8 + j : 4 * k - 7 + j, :], (SUB, LANES)) for j in range(4)]
        waiting = {}

        def reg(ref, row, j=0):
            return ref[row * SUB : (row + 1) * SUB, j * LANES : (j + 1) * LANES]

        def settle(r):
            best = waiting.pop(r)
            at = slice((r + 16) * SUB, (r + 17) * SUB)
            rm[at, :] = jnp.minimum(rm[at, :], best)

        for i in range(s * half, (s + 1) * half):
            rho = i - LEAD
            d = slice((rho - 4 * k + shift0) * SUB, (rho - 4 * k + shift0 + 1) * SUB)
            gs = [reg(g, rho + LEAD + j, j) for j in range(4)]
            prev = gc[d, :]
            one = [prev + gs[0], gs[0] + gs[1], gs[1] + gs[2], gs[2] + gs[3]]
            two = [a1c[0][d, :] + one[0], a1c[1][d, :] + one[1], one[0] + one[2], one[1] + one[3]]
            if last:
                three = [a2c[j][d, :] + two[j] for j in range(4)]
                for j in range(4):
                    r = rho - 7 + j
                    if r < 0 or r >= rows:
                        continue
                    row_value = three[j] + nbs[j]
                    col_value = three[j] + nab[(r + 16) * SUB : (r + 17) * SUB, :]
                    mins[j] = col_value if mins[j] is None else jnp.minimum(mins[j], col_value)
                    waiting[r] = jnp.minimum(waiting[r], row_value) if r in waiting else row_value
                    if j == 0:
                        settle(r)
            if k < steps - 1:
                gc[d, :] = gs[3]
                a1c[0][d, :] = one[2]
                a1c[1][d, :] = one[3]
                for j in range(4):
                    a2c[j][d, :] = two[j]
        for r in sorted(waiting):
            settle(r)
        return mins

    multiply(0, 0)
    multiply(0, 1)
    for k in range(steps):
        if k == steps - 1:
            p = lax.broadcasted_iota(jnp.int32, (SPAN // 2, LANES), 0)
            lane = lax.broadcasted_iota(jnp.int32, (SPAN // 2, LANES), 1)
            for j in range(4):
                close = (lane >= LANES - SUB) & (p < SUB * j + lane - (LANES - SUB))
                at = (7 - j - 4 * k + shift0) * SUB
                a2c[j][at : at + SPAN // 2, :] += jnp.where(close, pen_ref[0, 0], 0.0)
        mins = [None] * 4
        for s in range(2):
            if k + 1 < steps:
                multiply(k + 1, s)
            mins = combine(k, s, mins)
        if k >= 2:
            for j in range(4):
                t = 4 * k - 8 + j
                co_ref[t : t + 1, :] = jnp.min(mins[j], axis=0, keepdims=True)
    scale = 1.0 / (SPAN * width)
    ro_ref[...] = jnp.minimum(
        (jnp.min(rm[16 * SUB : (16 + rows) * SUB, :], axis=1, keepdims=True) + na_ref[...]) * scale, CEIL
    )
    co_ref[...] = jnp.minimum((co_ref[...] + nb_ref[...]) * scale, CEIL)


def meet(x_ext, y_ext, na, nb, pen):
    row_count = na.shape[0]
    col_count = nb.shape[0]
    width = x_ext.shape[1]
    rows = row_count // SUB
    tiles = col_count // LANES
    steps = (tiles + 8) // 4
    x_rows = (rows + 12) * SUB
    x_rows = -(-x_rows // 160) * 160
    nb_t = nb.reshape(HIGH, tiles, SUB).transpose(1, 0, 2).reshape(tiles, LANES)
    deep = (rows + 12 + 4 * steps) * SUB
    f32 = jnp.float32
    vm = functools.partial(pltpu.VMEM)
    scratch = [
        vm((x_rows + 16, width), f32),
        vm((col_count + SPAN + 2 * SUB, width), f32),
        vm((x_rows, SUB * width), jnp.bfloat16),
        vm((4 * steps * LANES, SUB * width), jnp.bfloat16),
        vm((x_rows + LEAD * SUB, 4 * LANES), f32),
        vm((x_rows + LEAD * SUB, 4 * LANES), f32),
    ] + [vm((deep, LANES), f32)] * 7 + [vm(((rows + 32) * SUB, LANES), f32)] * 2
    ro, co = pl.pallas_call(
        functools.partial(meet_kernel, rows, tiles),
        out_shape=(jax.ShapeDtypeStruct((row_count, 1), f32), jax.ShapeDtypeStruct((tiles, LANES), f32)),
        in_specs=[pl.BlockSpec(memory_space=pltpu.VMEM)] * 4 + [pl.BlockSpec(memory_space=pltpu.SMEM)],
        out_specs=[pl.BlockSpec(memory_space=pltpu.VMEM)] * 2,
        scratch_shapes=scratch,
        compiler_params=pltpu.CompilerParams(vmem_limit_bytes=48 * 1024 * 1024),
        cost_estimate=pl.CostEstimate(flops=2 * row_count * col_count * SUB * width, bytes_accessed=2 << 20, transcendentals=0),
    )(x_ext, y_ext, na[:, None], nb_t, pen)
    return ro[:, 0], co.reshape(tiles, HIGH, SUB).transpose(1, 0, 2).reshape(col_count)


def meeting(own_ext, own_norm, me, partner, target, axis_name, seg_count):
    far_ext = lax.dynamic_slice_in_dim(
        lax.all_gather(own_ext, axis_name, axis=0, tiled=True), target * own_ext.shape[0], own_ext.shape[0], 0
    )
    far_norm = lax.dynamic_index_in_dim(lax.all_gather(own_norm, axis_name, axis=0), target, 0, keepdims=False)
    half = seg_count // 2
    lower = me < partner
    x_ext = jnp.where(lower, far_ext[: half + SPAN], own_ext[half:])
    y_ext = jnp.where(lower, own_ext, far_ext)
    na = jnp.where(lower, far_norm[:half], own_norm[half:])
    nb = jnp.where(lower, own_norm, far_norm)
    pen = jnp.where(lower & (partner == me + 1), BIG, 0.0).astype(jnp.float32).reshape(1, 1)
    across, down = meet(x_ext, y_ext, na, nb, pen)
    capped = jnp.full((half,), CEIL, jnp.float32)
    kept = jnp.where(lower, down, jnp.concatenate([capped, across]))
    outgoing = jnp.where(lower, jnp.concatenate([across, capped]), down)
    arrived = lax.dynamic_index_in_dim(
        lax.all_gather(outgoing, axis_name, axis=0), target, 0, keepdims=False
    )
    return jnp.minimum(kept, arrived)


def per_device(beats, track_marks, valid_beats, pairing):
    seg_count = beats.shape[0]
    col_count = lax.axis_size("col")
    total = valid_beats.shape[0]
    me = lax.axis_index("row") * col_count + lax.axis_index("col")
    marks = track_marks.astype(jnp.bfloat16)
    head_beats, head_marks = from_behind((beats[:SPAN], marks[:SPAN]), ("row", "col"), -1)
    own_ext = jnp.concatenate([beats, head_beats], 0)
    mark_ext = jnp.concatenate([marks, head_marks], 0).astype(jnp.float32)
    crossed = window_sum(mark_ext, seg_count) - mark_ext[:seg_count]
    offsets = jnp.arange(seg_count, dtype=jnp.int32)
    valid_here = valid_beats[me]
    within = offsets + (SPAN - 1) < valid_here
    crossing = (valid_here == seg_count) & (me < total - 1)
    live = (within | crossing) & (crossed < 0.5)
    own_sq = jnp.sum(jnp.square(own_ext.astype(jnp.float32)), axis=1)
    own_norm = jnp.where(live, window_sum(own_sq, seg_count), BIG)
    first = pairing[0, me]
    second = pairing[1, me]
    a = meeting(own_ext, own_norm, me, first, first // col_count, "row", seg_count)
    b = meeting(own_ext, own_norm, me, second, second % col_count, "col", seg_count)
    return jnp.minimum(a, b)


def solution(mesh):
    placed = (P(("row", "col"), None), P(("row", "col")), P(), P())
    return jax.shard_map(
        per_device, mesh=mesh, in_specs=placed, out_specs=P(("row", "col")), check_vma=False
    )
```

time: 198 us -> 162 us (0.82)
  other arithmetic: 57.6 us -> 7.25 us
  Pallas kernels: 0 us -> 23.5 us
  waiting for transfers between devices: 27 us -> 44.3 us
  local copies, waits for them, and re-layouts: 16.1 us -> 5.97 us
  starting transfers between devices: 9.47 us -> 2.62 us
  loops' own time: 6.11 us -> 0 us
  matrix products: 4.11 us -> 0 us
    all_gather x0 -> x4, blocking collectives: none -> 56.1 us  [the longest x2 33.9 us: meeting(): lax.all_gather(own_norm, axis_name, axis=0)]
    unnamed x2 -> x0, blocking collectives: 54.3 us -> none
    add x42 -> x10, other arithmetic: 34.1 us -> 0.77 us  [window_sum(): layered = layered[:-window] + layered[window:]]
    pallas_call x0 -> x2, Pallas kernels: none -> 23.5 us  [meet(): pl.pallas_call(functools.partial(meet_kernel, rows, tiles), out_shape=(ja...]
    all_gather x2, waiting for transfers between devices: 19.8 us -> 42.9 us  [meeting(): lax.all_gather(own_ext, axis_name, axis=0, tiled=True)]
    reduce_min x12 -> x0, other arithmetic: 14.5 us -> none  [the longest x8 14.4 us: one_block(): return (jnp.min(masked, axis=1), jnp.min(masked, axis=0))]
    dynamic_slice x25 -> x5, local copies, waits for them, and re-layouts: 7.92 us -> 0.71 us  [the longest x1 0.62 us: per_device(): first = pairing[0, me]]
    all_to_all x2 -> x0, starting transfers between devices: 6.87 us -> none  [the longest x1 3.52 us: send_minima(): return lax.all_to_all(slots, 'row', split_axis=0, concat_axis=0, tiled=True)]
  transfers between devices with their start and end apart: 6 -> 4, of which waited for: 3 -> 2; matrix products, arithmetic and copies ran while one was open for 21% -> 5% of each run, Pallas kernels for 0% -> 0%
where the time goes in v1:
time: 162 us; the launch traced here: 161 us
  blocking collectives  56.1 us (35%)
  waiting for transfers between devices  44.3 us (27%)
  Pallas kernels  23.5 us (15%)
  between operations  21.4 us (13%)
  other arithmetic  7.25 us (4%)
  local copies, waits for them, and re-layouts  5.97 us (4%)
  starting transfers between devices  2.62 us (2%)
    all_gather x2, waiting for transfers between devices, meeting(): lax.all_gather(own_ext, axis_name, axis=0, tiled=True)  42.9 us
    all_gather x2, blocking collectives, meeting(): lax.all_gather(own_norm, axis_name, axis=0)  33.9 us
    pallas_call x2, Pallas kernels, meet(): pl.pallas_call(functools.partial(meet_kernel, rows, tiles), out_shape=(ja...  23.5 us
    all_gather x2, blocking collectives, meeting(): lax.all_gather(outgoing, axis_name, axis=0)  22.3 us
  transfers between devices with their start and end apart: 4, of which 2 were waited for; matrix products, arithmetic and copies ran while one was open for 5% of the time, Pallas kernels for 0%

profile of v1, /device:TPU:0, one launch (start us, length us, event | category | flops | bytes accessed | tf_op | source)
XLA Modules:
  0.0 161.2 jit_solution(7096961379521178496)
XLA Ops:
  6.5 0.8 slice.115
  7.3 1.3 collective-permute-start
  8.6 1.1 constant_dynamic-update-slice_fusion.1
  9.7 0.7 collective-permute-done
  10.4 0.8 copy-done
  11.2 0.7 all-gather.9.cloned.1.call-update
  12.0 1.3 collective-permute-start.1
  13.3 0.6 constant_dynamic-slice_fusion.4
  21.0 0.6 dynamic_slice.31
  22.7 1.4 multiply_reduce_fusion
  24.6 0.7 fusion.6
  25.3 19.9 %all-gather = f32[8192]{0:T(1024)S(1)} all-gather(f32[2048]{0:T(1024)S(1)} %get-tuple-element.13), channel_id=2, replica_groups=mesh['row'=4,'col'=8] {'row'}, dimensions={0}, use_global_device_ids=true | all-gather | bytes 40960 | tf_op jit(solution)/shard_map/all_gather | solution.py:196
  45.2 14.0 %all-gather.2 = f32[16384]{0:T(1024)S(1)} all-gather(f32[2048]{0:T(1024)S(1)} %get-tuple-element.13), channel_id=4, replica_groups=mesh['row'=4,'col'=8] {'col'}, dimensions={0}, use_global_device_ids=true | all-gather | bytes 73728 | tf_op jit(solution)/shard_map/all_gather | solution.py:196
  59.2 0.2 copy.21.na_ref
  60.0 0.7 select_bitcast_fusion.1
  60.8 0.3 copy.16.na_ref
  61.2 42.9 %all-gather.9.cloned.1.call-done = bf16[16896,128]{1,0:T(8,128)(2,1)} async-done(((bf16[2112,128]{1,0:T(8,128)(2,1)}), bf16[16896,128]{1,0:T(8,128)(2,1)}) %all-gather.9.cloned.1.call-update) | async-done | bytes 4325392 | tf_op jit(solution)/shard_map/all_gather | solution.py:194
  104.1 1.2 dynamic-slice_select_fusion.3
  105.3 1.5 dynamic-slice_select_fusion.1
  106.8 11.8 %shard_map.47 = (f32[1024,1]{1,0:T(8,128)S(1)}, f32[16,128]{1,0:T(8,128)S(1)}) custom-call(bf16[1088,128]{1,0:T(8,128)(2,1)S(1)} %get-tuple-element.19.x_ref, bf16[2112,128]{1,0:T(8,128)(2,1)S(1)} %get-tuple-element.17.y_ref, f32[1024,1]{1,0:T(8,128)S(1)} %copy.21.na_ref, f32[16,128]{1,0:T(8,128)S(1)} %copy.22.nb_ref, f32[1,1]{1,0:T(1,128)} %bitcast.15.pen_ref), custom_call_target="tpu_custom_call" | custom-call | flops 4294967296 | bytes 2097152 | tf_op jit(solution)/shard_map/pallas_call | solution.py:180
  119.1 14.2 %all-gather.3 = f32[16384]{0:T(1024)S(1)} all-gather(f32[2048]{0:T(1024)S(1)} %pad_select_fusion), channel_id=5, replica_groups=mesh['row'=4,'col'=8] {'col'}, dimensions={0}, use_global_device_ids=true | all-gather | bytes 73728 | tf_op jit(solution)/shard_map/all_gather | solution.py:209
  133.3 11.7 %shard_map.46 = (f32[1024,1]{1,0:T(8,128)S(1)}, f32[16,128]{1,0:T(8,128)S(1)}) custom-call(bf16[1088,128]{1,0:T(8,128)(2,1)S(1)} %get-tuple-element.18.x_ref, bf16[2112,128]{1,0:T(8,128)(2,1)S(1)} %get-tuple-element.16.y_ref, f32[1024,1]{1,0:T(8,128)S(1)} %copy.16.na_ref, f32[16,128]{1,0:T(8,128)S(1)} %copy.17.nb_ref, f32[1,1]{1,0:T(1,128)} %bitcast.6.pen_ref), custom_call_target="tpu_custom_call" | custom-call | flops 4294967296 | bytes 2097152 | tf_op jit(solution)/shard_map/pallas_call | solution.py:180
  145.5 8.1 %all-gather.1 = f32[8192]{0:T(1024)S(1)} all-gather(f32[2048]{0:T(1024)S(1)} %pad_select_fusion.1), channel_id=3, replica_groups=mesh['row'=4,'col'=8] {'row'}, dimensions={0}, use_global_device_ids=true | all-gather | bytes 40960 | tf_op jit(solution)/shard_map/all_gather | solution.py:209
  153.7 0.6 minimum_minimum_fusion
  (59 shorter events, 2.9 us)
Async XLA Ops:
  6.5 5.4 %copy-start.2 = (s32[2048]{0:T(1024)S(1)}, s32[2048]{0:T(1024)}, u32[]{:S(2)}) copy-start(s32[2048]{0:T(1024)} %param.5) | copy-start | bytes 24580
  6.5 6.8 %copy-start.3 = (s32[2,32]{1,0:T(2,128)S(1)}, s32[2,32]{1,0:T(2,128)}, u32[]{:S(2)}) copy-start(s32[2,32]{1,0:T(2,128)} %param.7) | copy-start | bytes 772
  6.5 14.4 %copy-start.4 = (s32[32]{0:T(128)S(1)}, s32[32]{0:T(128)}, u32[]{:S(2)}) copy-start(s32[32]{0:T(128)} %param.6) | copy-start | bytes 388
  6.5 54.7 %all-gather.7.cloned.1.call-start = ((), (), s32[]{:S(2)}) async-start(), calls=%async_computation | async-start | bytes 2703360 | tf_op jit(solution)/shard_map/all_gather | solution.py:194
  7.3 3.1 %collective-permute-start = (bf16[64,128]{1,0:T(8,128)(2,1)S(1)}, bf16[64,128]{1,0:T(8,128)(2,1)S(1)}, u32[]{:S(2)}, u32[]{:S(2)}) collective-permute-start(bf16[64,128]{1,0:T(8,128)(2,1)S(1)} %slice.115), channel_id=1, source_target_pairs={{1,0},{2,1},{3,2},{4,3},{5,4},{6,5},{7,6},{8,7},{9,8},{10,9},{11,1... | collective-permute-start | bytes 49160 | tf_op jit(solution)/shard_map/ppermute | solution.py:22
  10.4 0.8 copy-start
  11.2 92.9 %all-gather.9.cloned.1.call-start = ((), (), s32[]{:S(2)}) async-start(), calls=%async_computation.1 | async-start | bytes 4866048 | tf_op jit(solution)/shard_map/all_gather | solution.py:194
  12.0 10.2 %collective-permute-start.1 = (bf16[64]{0:T(256)(128)(2,1)S(1)}, bf16[64]{0:T(256)(128)(2,1)S(1)}, u32[]{:S(2)}, u32[]{:S(2)}) collective-permute-start(bf16[64]{0:T(256)(128)(2,1)S(1)} %slice.154), channel_id=1, source_target_pairs={{1,0},{2,1},{3,2},{4,3},{5,4},{6,5},{7,6},{8,7},{9,8},{10,9},{11,1... | collective-permute-start | bytes 392 | tf_op jit(solution)/shard_map/ppermute | solution.py:22
  19.6 84.5 %copy-start.1 = (bf16[2112,128]{1,0:T(8,128)(2,1)S(1)}, bf16[2112,128]{1,0:T(8,128)(2,1)}, u32[]{:S(2)}) copy-start(bf16[2112,128]{1,0:T(8,128)(2,1)} %copy-done) | copy-start | bytes 1622020
Sparse Core Ops, SparseCore 0:
  11.3 42.7 all-gather.6
  55.7 48.3 all-gather.8

commit v2 on v1

--- a/solution.py
+++ b/solution.py
@@ -189,11 +189,197 @@
     return ro[:, 0], co.reshape(tiles, HIGH, SUB).transpose(1, 0, 2).reshape(col_count)
 
 
-def meeting(own_ext, own_norm, me, partner, target, axis_name, seg_count):
-    far_ext = lax.dynamic_slice_in_dim(
-        lax.all_gather(own_ext, axis_name, axis=0, tiled=True), target * own_ext.shape[0], own_ext.shape[0], 0
+def gather_kernel(ext, norm, row_ext, row_norm, col_ext, col_norm, send, col_send, row_recv, col_recv):
+    row_size, col_size = lax.axis_size("row"), lax.axis_size("col")
+    row, col = lax.axis_index("row"), lax.axis_index("col")
+    chips = col_size // 2
+    chip, core = col // 2, col % 2
+    sibling = 2 * chip + 1 - core
+    has_right, has_left = chip + 1 < chips, chip > 0
+    barrier = pltpu.get_barrier_semaphore()
+
+    def greet(target):
+        pl.semaphore_signal(barrier, inc=1, device_id=target, device_id_type=pl.DeviceIdType.MESH)
+
+    for d in range(1, row_size):
+        greet((lax.rem(row + d, row_size), col))
+    for d in range(1, col_size):
+        greet((row, lax.rem(col + d, col_size)))
+    pl.semaphore_wait(barrier, row_size + col_size - 2)
+
+    def moves(origin, way, own):
+        slot = 2 * origin + core
+        target = (row, sibling if way == 2 else col + 2 - 4 * way)
+        return [
+            pltpu.make_async_remote_copy(
+                src_ref=whole if own else parts.at[slot],
+                dst_ref=parts.at[slot],
+                send_sem=col_send.at[n, way, origin],
+                recv_sem=col_recv.at[n, slot],
+                device_id=target,
+                device_id_type=pl.DeviceIdType.MESH,
+            )
+            for n, (whole, parts) in enumerate(((ext, col_ext), (norm, col_norm)))
+        ]
+
+    def arrivals(slot):
+        for n, (whole, parts) in enumerate(((ext, col_ext), (norm, col_norm))):
+            pltpu.make_async_remote_copy(
+                src_ref=whole,
+                dst_ref=parts.at[slot],
+                send_sem=col_send.at[n, 0, 0],
+                recv_sem=col_recv.at[n, slot],
+                device_id=(row, sibling),
+                device_id_type=pl.DeviceIdType.MESH,
+            ).wait_recv()
+
+    def start(origin, way, own=False):
+        for move in moves(origin, way, own):
+            move.start()
+
+    def sent(origin, way, own=False):
+        for move in moves(origin, way, own):
+            move.wait_send()
+
+    def row_moves(d):
+        target = lax.rem(row + d, row_size)
+        return [
+            pltpu.make_async_remote_copy(
+                src_ref=whole,
+                dst_ref=parts.at[row],
+                send_sem=send.at[n, d],
+                recv_sem=row_recv.at[n, d],
+                device_id=(target, col),
+                device_id_type=pl.DeviceIdType.MESH,
+            )
+            for n, (whole, parts) in enumerate(((ext, row_ext), (norm, row_norm)))
+        ]
+
+    pl.when(has_right)(lambda: start(chip, 0, True))
+    pl.when(has_left)(lambda: start(chip, 1, True))
+    for d in range(1, row_size):
+        for move in row_moves(d):
+            move.start()
+    start(chip, 2, True)
+    for s in range(1, chips):
+
+        @pl.when(chip - s >= 0)
+        def _():
+            arrivals(2 * (chip - s) + core)
+            pl.when(has_right)(lambda: start(chip - s, 0))
+            start(chip - s, 2)
+
+        @pl.when(chip + s < chips)
+        def _():
+            arrivals(2 * (chip + s) + core)
+            pl.when(has_left)(lambda: start(chip + s, 1))
+            start(chip + s, 2)
+
+    for origin in range(chips):
+        arrivals(2 * origin + 1 - core)
+    for d in range(1, row_size):
+        source = lax.rem(row + row_size - d, row_size)
+        for n, (whole, parts) in enumerate(((ext, row_ext), (norm, row_norm))):
+            pltpu.make_async_remote_copy(
+                src_ref=whole,
+                dst_ref=parts.at[source],
+                send_sem=send.at[n, d],
+                recv_sem=row_recv.at[n, d],
+                device_id=(source, col),
+                device_id_type=pl.DeviceIdType.MESH,
+            ).wait_recv()
+        for move in row_moves(d):
+            move.wait_send()
+    pl.when(has_right)(lambda: sent(chip, 0, True))
+    pl.when(has_left)(lambda: sent(chip, 1, True))
+    sent(chip, 2, True)
+    for s in range(1, chips):
+
+        @pl.when(chip - s >= 0)
+        def _():
+            pl.when(has_right)(lambda: sent(chip - s, 0))
+            sent(chip - s, 2)
+
+        @pl.when(chip + s < chips)
+        def _():
+            pl.when(has_left)(lambda: sent(chip + s, 1))
+            sent(chip + s, 2)
+
+
+def gather(ext, norm):
+    row_size, col_size = lax.axis_size("row"), lax.axis_size("col")
+    shapes = [
+        jax.ShapeDtypeStruct((size,) + v.shape, v.dtype) for size in (row_size, col_size) for v in (ext, norm)
+    ]
+    return pl.pallas_call(
+        gather_kernel,
+        out_shape=tuple(shapes),
+        in_specs=[pl.BlockSpec(memory_space=pl.ANY)] * 2,
+        out_specs=[pl.BlockSpec(memory_space=pl.ANY)] * 4,
+        scratch_shapes=[
+            pltpu.SemaphoreType.DMA((2, row_size)),
+            pltpu.SemaphoreType.DMA((2, 3, col_size // 2)),
+            pltpu.SemaphoreType.DMA((2, row_size)),
+            pltpu.SemaphoreType.DMA((2, col_size)),
+        ],
+        compiler_params=pltpu.CompilerParams(collective_id=0, has_side_effects=True),
+    )(ext, norm)
+
+
+def exchange_kernel(first, second, from_row, from_col, row_send, col_send, row_recv, col_recv):
+    row_size, col_size = lax.axis_size("row"), lax.axis_size("col")
+    row, col = lax.axis_index("row"), lax.axis_index("col")
+    barrier = pltpu.get_barrier_semaphore()
+    groups = (
+        (row, row_size, first, from_row, row_send, row_recv, lambda i: (i, col)),
+        (col, col_size, second, from_col, col_send, col_recv, lambda i: (row, i)),
     )
-    far_norm = lax.dynamic_index_in_dim(lax.all_gather(own_norm, axis_name, axis=0), target, 0, keepdims=False)
+    for me, size, _, _, _, _, place in groups:
+        for d in range(1, size):
+            pl.semaphore_signal(
+                barrier, inc=1, device_id=place(lax.rem(me + d, size)), device_id_type=pl.DeviceIdType.MESH
+            )
+    pl.semaphore_wait(barrier, row_size + col_size - 2)
+
+    def move(group, d, slot, target):
+        _, _, source, landing, send, recv, place = group
+        return pltpu.make_async_remote_copy(
+            src_ref=source,
+            dst_ref=landing.at[slot],
+            send_sem=send.at[d],
+            recv_sem=recv.at[d],
+            device_id=place(target),
+            device_id_type=pl.DeviceIdType.MESH,
+        )
+
+    for group in groups:
+        me, size = group[:2]
+        for d in range(1, size):
+            move(group, d, me, lax.rem(me + d, size)).start()
+    for group in groups:
+        me, size = group[:2]
+        for d in range(1, size):
+            source = lax.rem(me + size - d, size)
+            move(group, d, source, source).wait_recv()
+            move(group, d, me, lax.rem(me + d, size)).wait_send()
+
+
+def exchange(first, second):
+    row_size, col_size = lax.axis_size("row"), lax.axis_size("col")
+    sems = [pltpu.SemaphoreType.DMA((n,)) for n in (row_size, col_size)]
+    return pl.pallas_call(
+        exchange_kernel,
+        out_shape=tuple(jax.ShapeDtypeStruct((n,) + first.shape, first.dtype) for n in (row_size, col_size)),
+        in_specs=[pl.BlockSpec(memory_space=pltpu.VMEM)] * 2,
+        out_specs=[pl.BlockSpec(memory_space=pltpu.VMEM)] * 2,
+        scratch_shapes=sems + sems,
+        compiler_params=pltpu.CompilerParams(collective_id=1, has_side_effects=True),
+    )(first, second)
+
+
+def meeting(own_ext, own_norm, me, partner, target, far_exts, far_norms, seg_count):
+    far_ext = lax.dynamic_index_in_dim(far_exts, target, 0, keepdims=False)
+    far_norm = lax.dynamic_index_in_dim(far_norms, target, 0, keepdims=False).reshape(seg_count)
     half = seg_count // 2
     lower = me < partner
     x_ext = jnp.where(lower, far_ext[: half + SPAN], own_ext[half:])
@@ -205,10 +391,7 @@
     capped = jnp.full((half,), CEIL, jnp.float32)
     kept = jnp.where(lower, down, jnp.concatenate([capped, across]))
     outgoing = jnp.where(lower, jnp.concatenate([across, capped]), down)
-    arrived = lax.dynamic_index_in_dim(
-        lax.all_gather(outgoing, axis_name, axis=0), target, 0, keepdims=False
-    )
-    return jnp.minimum(kept, arrived)
+    return kept, outgoing.reshape(seg_count // LANES, LANES)
 
 
 def per_device(beats, track_marks, valid_beats, pairing):
@@ -230,9 +413,16 @@
     own_norm = jnp.where(live, window_sum(own_sq, seg_count), BIG)
     first = pairing[0, me]
     second = pairing[1, me]
-    a = meeting(own_ext, own_norm, me, first, first // col_count, "row", seg_count)
-    b = meeting(own_ext, own_norm, me, second, second % col_count, "col", seg_count)
-    return jnp.minimum(a, b)
+    to_row, to_col = first // col_count, second % col_count
+    row_ext, row_norm, col_ext, col_norm = gather(own_ext, own_norm.reshape(seg_count // LANES, LANES))
+    kept_a, out_a = meeting(own_ext, own_norm, me, first, to_row, row_ext, row_norm, seg_count)
+    kept_b, out_b = meeting(own_ext, own_norm, me, second, to_col, col_ext, col_norm, seg_count)
+    from_row, from_col = exchange(out_a, out_b)
+    near = jnp.minimum(
+        lax.dynamic_index_in_dim(from_row, to_row, 0, keepdims=False),
+        lax.dynamic_index_in_dim(from_col, to_col, 0, keepdims=False),
+    )
+    return jnp.minimum(jnp.minimum(kept_a, kept_b), near.reshape(seg_count))
 
 
 def solution(mesh):

time: 162 us -> 111 us (0.69)
  Pallas kernels: 23.5 us -> 82.2 us
  blocking collectives: 56.1 us -> 0 us
  waiting for transfers between devices: 44.3 us -> 0.01 us
  between operations: 21.4 us -> 7.47 us
  other arithmetic: 7.25 us -> 10.7 us
    pallas_call x0 -> x2, Pallas kernels: none -> 58.6 us  [the longest x1 49.4 us: gather(): pl.pallas_call(gather_kernel, out_shape=tuple(shapes), in_specs=[pl.Block...]
    all_gather x4 -> x0, blocking collectives: 56.1 us -> none  [the longest x2 33.9 us: meeting(): lax.all_gather(own_norm, axis_name, axis=0)]
    all_gather x2 -> x0, waiting for transfers between devices: 42.9 us -> none  [meeting(): lax.all_gather(own_ext, axis_name, axis=0, tiled=True)]
  transfers between devices with their start and end apart: 4 -> 2, of which waited for: 2 -> 0; matrix products, arithmetic and copies ran while one was open for 5% -> 4% of each run, Pallas kernels for 0% -> 0%
where the time goes in v2:
time: 111 us; the launch traced here: 110 us
  Pallas kernels  82.2 us (74%)
  other arithmetic  10.7 us (10%)
  between operations  7.47 us (7%)
  local copies, waits for them, and re-layouts  7.26 us (7%)
  starting transfers between devices  2.56 us (2%)
    pallas_call x1, Pallas kernels, gather(): pl.pallas_call(gather_kernel, out_shape=tuple(shapes), in_specs=[pl.Block...  49.4 us
    pallas_call x2, Pallas kernels, meet(): pl.pallas_call(functools.partial(meet_kernel, rows, tiles), out_shape=(ja...  23.6 us
    pallas_call x1, Pallas kernels, exchange(): pl.pallas_call(exchange_kernel, out_shape=tuple((jax.ShapeDtypeStruct((n,...  9.16 us
    ppermute x2, starting transfers between devices, from_behind(): return lax.ppermute(block, axis, route)  2.56 us
  transfers between devices with their start and end apart: 2, of which 0 were waited for; matrix products, arithmetic and copies ran while one was open for 4% of the time, Pallas kernels for 0%

profile of v2, /device:TPU:0, one launch (start us, length us, event | category | flops | bytes accessed | tf_op | source)
XLA Modules:
  0.0 110.2 jit_solution(15653542455089422218)
XLA Ops:
  0.0 0.7 slice.123
  0.7 1.3 %collective-permute-start = (bf16[64,128]{1,0:T(8,128)(2,1)S(1)}, bf16[64,128]{1,0:T(8,128)(2,1)S(1)}, u32[]{:S(2)}, u32[]{:S(2)}) collective-permute-start(bf16[64,128]{1,0:T(8,128)(2,1)S(1)} %slice.123), channel_id=1, source_target_pairs={{1,0},{2,1},{3,2},{4,3},{5,4},{6,5},{7,6},{8,7},{9,8},{10,9},{11,1... | collective-permute-start | bytes 49160 | tf_op jit(solution)/shard_map/ppermute | solution.py:22
  2.0 0.7 convert_element_type.9
  2.7 1.3 %collective-permute-start.1 = (bf16[64]{0:T(256)(128)(2,1)S(1)}, bf16[64]{0:T(256)(128)(2,1)S(1)}, u32[]{:S(2)}, u32[]{:S(2)}) collective-permute-start(bf16[64]{0:T(256)(128)(2,1)S(1)} %slice.164), channel_id=1, source_target_pairs={{1,0},{2,1},{3,2},{4,3},{5,4},{6,5},{7,6},{8,7},{9,8},{10,9},{11,1... | collective-permute-start | bytes 392 | tf_op jit(solution)/shard_map/ppermute | solution.py:22
  4.0 1.1 constant_dynamic-update-slice_fusion.1
  5.1 1.3 %constant_dynamic-slice_fusion.3 = (s32[1,1]{1,0:T(1,128)}, s32[1,1]{1,0:T(1,128)}) fusion(s32[2,32]{1,0:T(2,128)} %param.7, s32[]{:T(128)S(6)} %select_n.126), kind=kLoop, calls=%fused_computation.49 | loop fusion | bytes 20 | tf_op jit(solution)/shard_map/dynamic_slice | solution.py:415
  12.5 1.3 %dynamic_slice.32 = s32[1]{0:T(128)} dynamic-slice(s32[32]{0:T(128)} %param.6, s32[]{:T(128)S(6)} %select_n.126), dynamic_slice_sizes={1} | dynamic-slice | bytes 12 | tf_op jit(solution)/shard_map/dynamic_slice | solution.py:408
  15.5 0.4 multiply_reduce_fusion
  16.3 1.2 %bitcast_select_fusion.2 = (f32[16,128]{1,0:T(8,128)}, pred[2048]{0:T(1024)(128)(4,1)S(1)}, f32[2048]{0:T(1024)S(1)}) fusion(s32[]{:T(128)} %bitcast.1, pred[]{:T(512)S(6)} %and.31, f32[2112]{0:T(1024)S(1)} %maximum_convert_fusion, f32[2049]{0:T(1024)S(1)} %get-tuple-element.37, f32[2049]{0:T(1024)S(1)} %get-tuple-element.36, ...), kind=kLoop, calls=%fused_computation.28 | loop fusion | flops 22528 | bytes 59397 | tf_op jit(solution)/shard_map/jit(_where)/select_n | solution.py:413
  17.6 49.4 %shard_map.46 = (bf16[4,2112,128]{2,1,0:T(8,128)(2,1)}, f32[4,16,128]{2,1,0:T(8,128)}, bf16[8,2112,128]{2,1,0:T(8,128)(2,1)}, f32[8,16,128]{2,1,0:T(8,128)}) custom-call(bf16[2112,128]{1,0:T(8,128)(2,1)} %copy-done, f32[16,128]{1,0:T(8,128)} %get-tuple-element.25.norm), custom_call_target="tpu_custom_call" | custom-call | tf_op jit(solution)/shard_map/pallas_call | solution.py:314
  67.0 1.2 %fusion = (bf16[1088,128]{1,0:T(8,128)(2,1)S(1)}, bf16[1088,128]{1,0:T(8,128)(2,1)S(1)}) fusion(bf16[8,2112,128]{2,1,0:T(8,128)(2,1)} %get-tuple-element.19, s32[]{:T(128)S(6)} %select_n.146, pred[]{:T(512)S(6)} %lt.80, bf16[2112,128]{1,0:T(8,128)(2,1)} %copy-done, bf16[4,2112,128]{2,1,0:T(8,128)(2,1)} %get-tuple-element.15, s32[]{:T(128)S(6)} %select_n.131, ...), kind=kLoop, calls=%fused_computation.4 | loop fusion | flops 278528 | bytes 1392650 | tf_op jit(solution)/shard_map/jit(_where)/select_n | solution.py:385
  68.1 1.5 %bitcast_select_fusion = (bf16[2112,128]{1,0:T(8,128)(2,1)S(1)}, bf16[2112,128]{1,0:T(8,128)(2,1)S(1)}) fusion(bf16[2112,128]{1,0:T(8,128)(2,1)} %copy-done, bf16[8,2112,128]{2,1,0:T(8,128)(2,1)} %get-tuple-element.19, s32[]{:T(128)S(6)} %select_n.146, pred[]{:T(512)S(6)} %lt.80, bf16[4,2112,128]{2,1,0:T(8,128)(2,1)} %get-tuple-element.15, s32[]{:T(128)S(6)} %select_n.131, ...), kind=kLoop, calls=%fused_computation.1 | loop fusion | flops 540672 | bytes 2703370 | tf_op jit(solution)/shard_map/jit(_where)/select_n | solution.py:386
  69.7 0.7 constant_dynamic-slice_fusion
  70.4 1.3 %fusion.8 = (f32[1024]{0:T(1024)S(1)}, f32[1024]{0:T(1024)S(1)}) fusion(f32[8,16,128]{2,1,0:T(8,128)} %get-tuple-element.20, s32[]{:T(128)S(6)} %select_n.146, pred[]{:T(512)S(6)} %lt.80, f32[2048]{0:T(1024)S(1)} %get-tuple-element.27, pred[2048]{0:T(1024)(128)(4,1)S(1)} %get-tuple-element.26, pred[]{:T(512)S(6)} %and.31, s32[]{:T(128)} %bitcast.1, ...), kind=kLoop, calls=%fused_computation.38 | loop fusion | flops 8192 | bytes 21519 | tf_op jit(solution)/shard_map/jit(_where)/select_n | solution.py:387
  71.9 0.2 copy.8.na_ref
  72.6 0.7 select_bitcast_fusion
  73.4 11.7 %shard_map.47 = (f32[1024,1]{1,0:T(8,128)S(1)}, f32[16,128]{1,0:T(8,128)S(1)}) custom-call(bf16[1088,128]{1,0:T(8,128)(2,1)S(1)} %get-tuple-element.31.x_ref, bf16[2112,128]{1,0:T(8,128)(2,1)S(1)} %get-tuple-element.29.y_ref, f32[1024,1]{1,0:T(8,128)S(1)} %copy.8.na_ref, f32[16,128]{1,0:T(8,128)S(1)} %copy.9.nb_ref, f32[1,1]{1,0:T(1,128)} %bitcast.11.pen_ref), custom_call_target="tpu_custom_call" | custom-call | flops 4294967296 | bytes 2097152 | tf_op jit(solution)/shard_map/pallas_call | solution.py:180
  85.4 0.2 copy.15.na_ref
  85.8 11.9 %shard_map.48 = (f32[1024,1]{1,0:T(8,128)S(1)}, f32[16,128]{1,0:T(8,128)S(1)}) custom-call(bf16[1088,128]{1,0:T(8,128)(2,1)S(1)} %get-tuple-element.30.x_ref, bf16[2112,128]{1,0:T(8,128)(2,1)S(1)} %get-tuple-element.28.y_ref, f32[1024,1]{1,0:T(8,128)S(1)} %copy.15.na_ref, f32[16,128]{1,0:T(8,128)S(1)} %copy.16.nb_ref, f32[1,1]{1,0:T(1,128)} %bitcast.22.pen_ref), custom_call_target="tpu_custom_call" | custom-call | flops 4294967296 | bytes 2097152 | tf_op jit(solution)/shard_map/pallas_call | solution.py:180
  98.3 0.2 reduce.1
  98.5 0.6 select_bitcast_fusion.3.first
  99.1 0.6 select_bitcast_fusion.2.second
  99.7 9.2 %shard_map.49 = (f32[4,16,128]{2,1,0:T(8,128)}, f32[8,16,128]{2,1,0:T(8,128)}) custom-call(f32[16,128]{1,0:T(8,128)} %select_bitcast_fusion.3.first, f32[16,128]{1,0:T(8,128)} %select_bitcast_fusion.2.second), custom_call_target="tpu_custom_call" | custom-call | tf_op jit(solution)/shard_map/pallas_call | solution.py:370
  108.8 1.3 %bitcast_minimum_fusion = f32[2048]{0:T(1024)} fusion(f32[8,16,128]{2,1,0:T(8,128)} %get-tuple-element.24, s32[]{:T(128)S(6)} %select_n.146, f32[4,16,128]{2,1,0:T(8,128)} %get-tuple-element.23, s32[]{:T(128)S(6)} %select_n.131, f32[2048]{0:T(1024)S(1)} %reshape.78, f32[1024]{0:T(1024)S(1)} %reduce.1, f32[2048]{0:T(1024)S(1)} %reshape.73, f32[1024]{0:T(1024)S(1)} %reduce, ...), kind=kLoop, calls=%fused_computation.27 | loop fusion | flops 10240 | bytes 49162 | tf_op jit(solution)/shard_map/min | solution.py:425
  (36 shorter events, 2.7 us)
Async XLA Ops:
  0.7 14.7 %collective-permute-start = (bf16[64,128]{1,0:T(8,128)(2,1)S(1)}, bf16[64,128]{1,0:T(8,128)(2,1)S(1)}, u32[]{:S(2)}, u32[]{:S(2)}) collective-permute-start(bf16[64,128]{1,0:T(8,128)(2,1)S(1)} %slice.123), channel_id=1, source_target_pairs={{1,0},{2,1},{3,2},{4,3},{5,4},{6,5},{7,6},{8,7},{9,8},{10,9},{11,1... | collective-permute-start | bytes 49160 | tf_op jit(solution)/shard_map/ppermute | solution.py:22
  2.7 12.3 %collective-permute-start.1 = (bf16[64]{0:T(256)(128)(2,1)S(1)}, bf16[64]{0:T(256)(128)(2,1)S(1)}, u32[]{:S(2)}, u32[]{:S(2)}) collective-permute-start(bf16[64]{0:T(256)(128)(2,1)S(1)} %slice.164), channel_id=1, source_target_pairs={{1,0},{2,1},{3,2},{4,3},{5,4},{6,5},{7,6},{8,7},{9,8},{10,9},{11,1... | collective-permute-start | bytes 392 | tf_op jit(solution)/shard_map/ppermute | solution.py:22
  15.5 2.1 %copy-start = (bf16[2112,128]{1,0:T(8,128)(2,1)}, bf16[2112,128]{1,0:T(8,128)(2,1)S(1)}, u32[]{:S(2)}) copy-start(bf16[2112,128]{1,0:T(8,128)(2,1)S(1)} %constant_dynamic-update-slice_fusion.ext) | copy-start | bytes 1622020

commit v3 on v2

--- a/solution.py
+++ b/solution.py
@@ -26,9 +26,9 @@
     layered = values
     window = 1
     while window < SPAN:
-        layered = layered[:-window] + layered[window:]
+        layered = layered[:, :-window] + layered[:, window:]
         window = window * 2
-    return layered[:count]
+    return layered[:, :count]
 
 
 def meet_kernel(
@@ -403,14 +403,15 @@
     head_beats, head_marks = from_behind((beats[:SPAN], marks[:SPAN]), ("row", "col"), -1)
     own_ext = jnp.concatenate([beats, head_beats], 0)
     mark_ext = jnp.concatenate([marks, head_marks], 0).astype(jnp.float32)
-    crossed = window_sum(mark_ext, seg_count) - mark_ext[:seg_count]
+    own_sq = jnp.sum(jnp.square(own_ext.astype(jnp.float32)), axis=1)
+    marked, norms = window_sum(jnp.stack([mark_ext, own_sq]), seg_count)
+    crossed = marked - mark_ext[:seg_count]
     offsets = jnp.arange(seg_count, dtype=jnp.int32)
     valid_here = valid_beats[me]
     within = offsets + (SPAN - 1) < valid_here
     crossing = (valid_here == seg_count) & (me < total - 1)
     live = (within | crossing) & (crossed < 0.5)
-    own_sq = jnp.sum(jnp.square(own_ext.astype(jnp.float32)), axis=1)
-    own_norm = jnp.where(live, window_sum(own_sq, seg_count), BIG)
+    own_norm = jnp.where(live, norms, BIG)
     first = pairing[0, me]
     second = pairing[1, me]
     to_row, to_col = first // col_count, second % col_count

time: 111 us -> 112 us (level)
  no operation moved by 1% of the time
where the time goes in v3:
time: 112 us; the launch traced here: 111 us
  Pallas kernels  82.2 us (73%)
  other arithmetic  11.3 us (10%)
  between operations  7.63 us (7%)
  local copies, waits for them, and re-layouts  7.33 us (7%)
  starting transfers between devices  2.56 us (2%)
    pallas_call x1, Pallas kernels, gather(): pl.pallas_call(gather_kernel, out_shape=tuple(shapes), in_specs=[pl.Block...  49.4 us
    pallas_call x2, Pallas kernels, meet(): pl.pallas_call(functools.partial(meet_kernel, rows, tiles), out_shape=(ja...  23.7 us
    pallas_call x1, Pallas kernels, exchange(): pl.pallas_call(exchange_kernel, out_shape=tuple((jax.ShapeDtypeStruct((n,...  9.15 us
    ppermute x2, starting transfers between devices, from_behind(): return lax.ppermute(block, axis, route)  2.56 us
  transfers between devices with their start and end apart: 2, of which 0 were waited for; matrix products, arithmetic and copies ran while one was open for 4% of the time, Pallas kernels for 0%

profile of v3, /device:TPU:0, one launch (start us, length us, event | category | flops | bytes accessed | tf_op | source)
XLA Modules:
  0.0 111.0 jit_solution(16411924237842264619)
XLA Ops:
  0.0 0.7 slice.85
  0.7 1.3 %collective-permute-start = (bf16[64,128]{1,0:T(8,128)(2,1)S(1)}, bf16[64,128]{1,0:T(8,128)(2,1)S(1)}, u32[]{:S(2)}, u32[]{:S(2)}) collective-permute-start(bf16[64,128]{1,0:T(8,128)(2,1)S(1)} %slice.85), channel_id=1, source_target_pairs={{1,0},{2,1},{3,2},{4,3},{5,4},{6,5},{7,6},{8,7},{9,8},{10,9},{11,1... | collective-permute-start | bytes 49160 | tf_op jit(solution)/shard_map/ppermute | solution.py:22
  2.0 0.7 fusion.17
  2.7 1.3 %collective-permute-start.1 = (bf16[64]{0:T(256)(128)(2,1)S(1)}, bf16[64]{0:T(256)(128)(2,1)S(1)}, u32[]{:S(2)}, u32[]{:S(2)}) collective-permute-start(bf16[64]{0:T(256)(128)(2,1)S(1)} %slice.112), channel_id=1, source_target_pairs={{1,0},{2,1},{3,2},{4,3},{5,4},{6,5},{7,6},{8,7},{9,8},{10,9},{11,1... | collective-permute-start | bytes 392 | tf_op jit(solution)/shard_map/ppermute | solution.py:22
  4.0 1.1 constant_dynamic-update-slice_fusion.1
  5.1 1.3 %constant_dynamic-slice_fusion.3 = (s32[1,1]{1,0:T(1,128)}, s32[1,1]{1,0:T(1,128)}) fusion(s32[2,32]{1,0:T(2,128)} %param.7, s32[]{:T(128)S(6)} %select_n.126), kind=kLoop, calls=%fused_computation.47 | loop fusion | bytes 20 | tf_op jit(solution)/shard_map/dynamic_slice | solution.py:416
  12.6 1.3 %dynamic_slice.32 = s32[1]{0:T(128)} dynamic-slice(s32[32]{0:T(128)} %param.6, s32[]{:T(128)S(6)} %select_n.126), dynamic_slice_sizes={1} | dynamic-slice | bytes 12 | tf_op jit(solution)/shard_map/dynamic_slice | solution.py:410
  15.3 0.4 multiply_reduce_fusion
  16.3 1.3 %fusion.9.norm = f32[16,128]{1,0:T(8,128)} fusion(f32[16,128]{1,0:T(8,128)S(1)} %bitcast.64, f32[16,128]{1,0:T(8,128)S(1)} %bitcast.66, s32[]{:T(128)} %bitcast.1, pred[]{:T(512)S(6)} %and.31, bf16[2048]{0:T(1024)(128)(2,1)S(1)} %get-tuple-element.32), kind=kLoop, calls=%fused_computation.30 | loop fusion | flops 20480 | bytes 28677 | tf_op jit(solution)/shard_map/jit(_where)/select_n | solution.py:414
  17.6 49.4 %shard_map.46 = (bf16[4,2112,128]{2,1,0:T(8,128)(2,1)}, f32[4,16,128]{2,1,0:T(8,128)}, bf16[8,2112,128]{2,1,0:T(8,128)(2,1)}, f32[8,16,128]{2,1,0:T(8,128)}) custom-call(bf16[2112,128]{1,0:T(8,128)(2,1)} %copy-done, f32[16,128]{1,0:T(8,128)} %fusion.9.norm), custom_call_target="tpu_custom_call" | custom-call | tf_op jit(solution)/shard_map/pallas_call | solution.py:314
  67.0 1.2 %fusion = (bf16[1088,128]{1,0:T(8,128)(2,1)S(1)}, bf16[1088,128]{1,0:T(8,128)(2,1)S(1)}) fusion(bf16[8,2112,128]{2,1,0:T(8,128)(2,1)} %get-tuple-element.19, s32[]{:T(128)S(6)} %select_n.146, pred[]{:T(512)S(6)} %lt.84, bf16[2112,128]{1,0:T(8,128)(2,1)} %copy-done, bf16[4,2112,128]{2,1,0:T(8,128)(2,1)} %get-tuple-element.15, s32[]{:T(128)S(6)} %select_n.131, ...), kind=kLoop, calls=%fused_computation.4 | loop fusion | flops 278528 | bytes 1392650 | tf_op jit(solution)/shard_map/jit(_where)/select_n | solution.py:385
  68.2 1.5 %bitcast_select_fusion = (bf16[2112,128]{1,0:T(8,128)(2,1)S(1)}, bf16[2112,128]{1,0:T(8,128)(2,1)S(1)}) fusion(bf16[2112,128]{1,0:T(8,128)(2,1)} %copy-done, bf16[8,2112,128]{2,1,0:T(8,128)(2,1)} %get-tuple-element.19, s32[]{:T(128)S(6)} %select_n.146, pred[]{:T(512)S(6)} %lt.84, bf16[4,2112,128]{2,1,0:T(8,128)(2,1)} %get-tuple-element.15, s32[]{:T(128)S(6)} %select_n.131, ...), kind=kLoop, calls=%fused_computation.1 | loop fusion | flops 540672 | bytes 2703370 | tf_op jit(solution)/shard_map/jit(_where)/select_n | solution.py:386
  69.7 0.7 constant_dynamic-slice_fusion
  70.4 1.4 %fusion.10 = (f32[1024]{0:T(1024)S(1)}, f32[1024]{0:T(1024)S(1)}) fusion(f32[8,16,128]{2,1,0:T(8,128)} %get-tuple-element.20, s32[]{:T(128)S(6)} %select_n.146, pred[]{:T(512)S(6)} %lt.84, f32[2048]{0:T(1024)S(1)} %bitcast.65, f32[2048]{0:T(1024)S(1)} %get-tuple-element.31, f32[2048]{0:T(1024)S(1)} %bitcast.67, pred[]{:T(512)S(6)} %and.31, s32[]{:T(128)} %bitcast.1), kind=kLoop, calls=%fused_computation.34 | loop fusion | flops 9216 | bytes 24586 | tf_op jit(solution)/shard_map/jit(_where)/select_n | solution.py:387
  71.8 0.7 fusion.13
  72.5 0.2 copy.8.na_ref
  73.3 0.7 select_bitcast_fusion
  74.3 11.7 %shard_map.47 = (f32[1024,1]{1,0:T(8,128)S(1)}, f32[16,128]{1,0:T(8,128)S(1)}) custom-call(bf16[1088,128]{1,0:T(8,128)(2,1)S(1)} %get-tuple-element.36.x_ref, bf16[2112,128]{1,0:T(8,128)(2,1)S(1)} %get-tuple-element.34.y_ref, f32[1024,1]{1,0:T(8,128)S(1)} %copy.8.na_ref, f32[16,128]{1,0:T(8,128)S(1)} %copy.9.nb_ref, f32[1,1]{1,0:T(1,128)} %bitcast.15.pen_ref), custom_call_target="tpu_custom_call" | custom-call | flops 4294967296 | bytes 2097152 | tf_op jit(solution)/shard_map/pallas_call | solution.py:180
  86.3 0.2 copy.15.na_ref
  86.7 11.9 %shard_map.48 = (f32[1024,1]{1,0:T(8,128)S(1)}, f32[16,128]{1,0:T(8,128)S(1)}) custom-call(bf16[1088,128]{1,0:T(8,128)(2,1)S(1)} %get-tuple-element.35.x_ref, bf16[2112,128]{1,0:T(8,128)(2,1)S(1)} %get-tuple-element.33.y_ref, f32[1024,1]{1,0:T(8,128)S(1)} %copy.15.na_ref, f32[16,128]{1,0:T(8,128)S(1)} %copy.16.nb_ref, f32[1,1]{1,0:T(1,128)} %bitcast.26.pen_ref), custom_call_target="tpu_custom_call" | custom-call | flops 4294967296 | bytes 2097152 | tf_op jit(solution)/shard_map/pallas_call | solution.py:180
  99.3 0.6 select_bitcast_fusion.3.first
  100.0 0.6 select_bitcast_fusion.2.second
  100.6 9.1 %shard_map.49 = (f32[4,16,128]{2,1,0:T(8,128)}, f32[8,16,128]{2,1,0:T(8,128)}) custom-call(f32[16,128]{1,0:T(8,128)} %select_bitcast_fusion.3.first, f32[16,128]{1,0:T(8,128)} %select_bitcast_fusion.2.second), custom_call_target="tpu_custom_call" | custom-call | tf_op jit(solution)/shard_map/pallas_call | solution.py:370
  109.7 1.3 %bitcast_minimum_fusion = f32[2048]{0:T(1024)} fusion(f32[8,16,128]{2,1,0:T(8,128)} %get-tuple-element.24, s32[]{:T(128)S(6)} %select_n.146, f32[4,16,128]{2,1,0:T(8,128)} %get-tuple-element.23, s32[]{:T(128)S(6)} %select_n.131, f32[2048]{0:T(1024)S(1)} %reshape.101, f32[1024]{0:T(1024)S(1)} %reduce.3, f32[2048]{0:T(1024)S(1)} %reshape.96, ...), kind=kLoop, calls=%fused_computation.22 | loop fusion | flops 10240 | bytes 49162 | tf_op jit(solution)/shard_map/min | solution.py:426
  (36 shorter events, 2.7 us)
Async XLA Ops:
  0.7 14.6 %collective-permute-start = (bf16[64,128]{1,0:T(8,128)(2,1)S(1)}, bf16[64,128]{1,0:T(8,128)(2,1)S(1)}, u32[]{:S(2)}, u32[]{:S(2)}) collective-permute-start(bf16[64,128]{1,0:T(8,128)(2,1)S(1)} %slice.85), channel_id=1, source_target_pairs={{1,0},{2,1},{3,2},{4,3},{5,4},{6,5},{7,6},{8,7},{9,8},{10,9},{11,1... | collective-permute-start | bytes 49160 | tf_op jit(solution)/shard_map/ppermute | solution.py:22
  2.7 12.5 %collective-permute-start.1 = (bf16[64]{0:T(256)(128)(2,1)S(1)}, bf16[64]{0:T(256)(128)(2,1)S(1)}, u32[]{:S(2)}, u32[]{:S(2)}) collective-permute-start(bf16[64]{0:T(256)(128)(2,1)S(1)} %slice.112), channel_id=1, source_target_pairs={{1,0},{2,1},{3,2},{4,3},{5,4},{6,5},{7,6},{8,7},{9,8},{10,9},{11,1... | collective-permute-start | bytes 392 | tf_op jit(solution)/shard_map/ppermute | solution.py:22
  15.3 2.3 %copy-start = (bf16[2112,128]{1,0:T(8,128)(2,1)}, bf16[2112,128]{1,0:T(8,128)(2,1)S(1)}, u32[]{:S(2)}) copy-start(bf16[2112,128]{1,0:T(8,128)(2,1)S(1)} %constant_dynamic-update-slice_fusion.ext) | copy-start | bytes 1622020
